TPU v7x, 32 devices: a whole 2x2x4 slice. The times are simulated.
32 devices in a mesh: ga: 2 (over y), col: 16 (over z, x, core).
Axes of the slice: x: 2, y: 2, z: 4, core: 2. Of those that a mesh axis runs over, the one named last changes fastest.
Arguments:
- query_nope: bfloat16 [128, 4096], P(('ga', 'col')), parts along dimension 0, may hold values from -6 to 6
- query_rope: bfloat16 [128, 2048], P(('ga', 'col')), parts along dimension 0, may hold values from -104 to 104, as said below
- cache: bfloat16 [8192, 576], P(('ga', 'col')), parts along dimension 0, may hold values from -6 to 6, as said below
- key_docs: int32 [8192], P(('ga', 'col')), parts along dimension 0, may hold values from 0 to 7, as said below
- query_docs: int32 [128], P(('ga', 'col')), parts along dimension 0, may hold values from 0 to 7, as said below
- query_pos: int32 [128], P(('ga', 'col')), parts along dimension 0, may hold values from 1 to 4095, as said below
- w_uk: bfloat16 [512, 4096], replicated, may hold values from -0.25 to 0.25
- w_uv: bfloat16 [512, 4096], replicated, may hold values from -0.25 to 0.25
Outputs:
- attended: bfloat16 [128, 4096], P(('ga', 'col')), parts along dimension 0
There are 2 independent parts, one for each index of `ga`. A program takes and returns all parts, laid end to end along the dimension named above; an argument that names none is the same for every part. Nothing has to cross between parts.
Inputs may be any that keep to these rules, and one draw needn't show every extreme that they name: `key_docs`: ids start at 0 and never fall along the cache; a document is a run of equal ids; eight documents. query_docs[i] equals key_docs[query_pos[i]]. `query_pos`: a position from 1 to 4095, never the first token of a document. `query_rope`: real values. `cache`: real values.
All inputs are finite; a program needn't handle non-finite values.
Results may differ from a plain program's by a relative error of at most 0.001.
Values may be sent and summed in bfloat16 or wider, within the bound.
A program may use at most 192 MiB of HBM per device.

v0:
```python
import math

import jax
import jax.numpy as jnp
from jax import lax
from jax.sharding import PartitionSpec as P

H = 32
DN = 128
DR = 64
DV = 128
R = 512


def shards(query_nope, query_rope, cache, key_docs, query_docs, query_pos, w_uk, w_uv):
    scale = 1.0 / math.sqrt(DN + DR)
    highest = lax.Precision.HIGHEST
    own_rows = query_nope.shape[0]
    q_flat = query_nope.astype(jnp.float32).reshape(own_rows, H, DN)
    absorbed = jnp.einsum(
        "qhd,rhd->qhr", q_flat, w_uk.astype(jnp.float32).reshape(R, H, DN), precision=highest
    )
    q_turn = query_rope.reshape(own_rows, H, DR).astype(jnp.float32)
    q_whole = jnp.concatenate([absorbed, q_turn], axis=2).reshape(own_rows * H, R + DR)
    row_docs = jnp.repeat(query_docs, H)
    row_pos = jnp.repeat(query_pos, H)
    rows_all = own_rows * H
    best = jnp.full((rows_all,), -1e30, jnp.float32)
    piece = lax.all_gather(cache, "col", axis=0, tiled=True)
    piece_docs = lax.all_gather(key_docs, "col", axis=0, tiled=True)
    count = piece.shape[0]
    wide_piece = piece.astype(jnp.float32)
    scores = jnp.einsum("rc,kc->rk", q_whole, wide_piece, precision=highest) * scale
    key_place = jnp.arange(count, dtype=jnp.int32)
    visible = (piece_docs[None, :] == row_docs[:, None]) & (key_place[None, :] <= row_pos[:, None])
    scores = jnp.where(visible, scores, -1e30)
    new_best = jnp.maximum(best, jnp.max(scores, axis=1))
    weights = jnp.where(visible, jnp.exp(scores - new_best[:, None]), 0.0)
    total = jnp.sum(weights, axis=1)
    added = jnp.dot(weights, wide_piece[:, :R], precision=highest)
    accum = added
    best, total, accum = (new_best, total, accum)
    mixed = (accum / total[:, None]).reshape(own_rows, H, R)
    result = jnp.einsum(
        "qhr,rhv->qhv", mixed, w_uv.reshape(R, H, DV).astype(jnp.float32), precision=highest
    )
    return result.reshape(own_rows, H * DV).astype(jnp.bfloat16)


def solution(mesh):
    placed = (
        P(("ga", "col"), None),
        P(("ga", "col"), None),
        P(("ga", "col"), None),
        P(("ga", "col")),
        P(("ga", "col")),
        P(("ga", "col")),
        P(),
        P(),
    )
    return jax.shard_map(
        shards, mesh=mesh, in_specs=placed, out_specs=P(("ga", "col"), None), check_vma=False
    )
```

profile of v0, /device:TPU:0, one launch (start us, length us, event | category | flops | bytes accessed | tf_op | source)
XLA Modules:
  0.0 88.0 jit_solution(14045177649011529404)
XLA Ops:
  6.5 0.0 copy-start
  6.5 0.0 all-gather.3.cloned.1.call-start
  6.5 0.7 all-gather.3.cloned.1.call-update
  7.3 0.7 broadcast_in_dim.20
  8.0 0.1 eq.16
  8.1 0.7 broadcast_in_dim.21
  8.8 0.1 le.16
  8.9 0.8 reshape.32
  9.7 0.0 copy-done
  9.7 0.0 copy-start.2
  9.8 3.4 %fusion.11 = f32[4,32,512]{2,0,1:T(4,128)S(1)} fusion(bf16[4,4096]{1,0:T(4,128)(2,1)S(1)} %copy-done, bf16[512,4096]{1,0:T(8,128)(2,1)} %param.14), kind=kOutput, calls=%fused_computation.14 | convolution fusion | flops 16777216 | bytes 4489216 | tf_op jit(solution)/shard_map/qhd,rhd->qhr/dot_general | solution.py:20
  13.1 0.1 pad_maximum_fusion
  13.3 0.0 copy-done.2
  13.3 23.2 %all-gather = s32[16,1,256]{2,1,0:T(1,128)S(1)} all-gather(s32[1,1,256]{2,1,0:T(1,128)S(1)} %bitcast.40), channel_id=1, replica_groups=mesh['ga'=2,'col'=16] {'col'}, dimensions={0}, use_global_device_ids=true | all-gather | bytes 17408 | tf_op jit(solution)/shard_map/all_gather | solution.py:30
  36.5 31.8 %all-gather.3.cloned.1.call-done = bf16[4096,576]{0,1:T(8,128)(2,1)} async-done(((bf16[256,576]{0,1:T(8,128)(2,1)}), bf16[4096,576]{0,1:T(8,128)(2,1)}) %all-gather.3.cloned.1.call-update) | async-done | bytes 4718608 | tf_op jit(solution)/shard_map/all_gather | solution.py:29
  68.3 0.0 slice-start
  68.3 5.0 %fusion.31 = (f32[128]{0:T(128)S(1)}, f32[128,4096]{1,0:T(8,128)S(1)}) fusion(f32[128,576]{1,0:T(8,128)S(1)} %bitcast.35, bf16[4096,576]{0,1:T(8,128)(2,1)} %all-gather.3.cloned.1.call-done, s32[128]{0:T(128)S(1)} %le.16, s32[128]{0:T(128)S(1)} %eq.16, s32[4096]{0:T(1024)S(1)} %bitcast.37), kind=kOutput, calls=%fused_computation.28 | convolution fusion | flops 3627024384 | bytes 7128576 | tf_op jit(solution)/shard_map/rc,kc->rk/dot_general | solution.py:33
  73.3 0.8 fusion.10
  74.0 0.0 slice-done
  74.1 0.0 slice-done.1
  74.1 0.0 copy-start.1
  74.1 4.3 %fusion.14 = f32[128,512]{1,0:T(8,128)S(1)} fusion(bf16[4096,576]{0,1:T(8,128)(2,1)S(1)} %bitcast.42, f32[128,4096]{1,0:T(8,128)S(1)} %get-tuple-element.6, f32[128]{0:T(128)S(1)} %broadcast_maximum_fusion, s32[128]{0:T(128)S(1)} %le.16, s32[4096]{0:T(1024)S(1)} %bitcast.39, s32[128]{0:T(128)S(1)} %eq.16, f32[128]{0:T(128)S(1)} %fusion.10), kind=kOutput, calls=%fused_computation.15 | convolution fusion | flops 3223912448 | bytes 6572032 | tf_op jit(solution)/shard_map/dot_general | solution.py:40
  78.4 0.0 copy-done.1
  78.4 2.8 %fusion.20 = bf16[4,4096]{1,0:T(4,128)(2,1)} fusion(f32[4,32,512]{2,1,0:T(8,128)S(1)} %bitcast.36, bf16[512,4096]{1,0:T(8,128)(2,1)S(1)} %copy-done.1), kind=kOutput, calls=%fused_computation.17 | convolution fusion | flops 100679680 | bytes 4489216 | tf_op jit(solution)/shard_map/qhr,rhv->qhv/dot_general | solution.py:44
  (5 shorter events, 0.1 us)
Async XLA Ops:
  6.5 3.2 %copy-start = (bf16[4,4096]{1,0:T(4,128)(2,1)S(1)}, bf16[4,4096]{1,0:T(4,128)(2,1)}, u32[]{:S(2)}) copy-start(bf16[4,4096]{1,0:T(4,128)(2,1)} %param.8) | copy-start | bytes 98308
  6.5 61.8 %all-gather.3.cloned.1.call-start = ((), (), s32[]{:S(2)}) async-start(), calls=%async_computation | async-start | bytes 5013504 | tf_op jit(solution)/shard_map/all_gather | solution.py:29
  9.7 3.5 %copy-start.2 = (s32[256]{0:T(256)S(1)}, s32[256]{0:T(256)}, u32[]{:S(2)}) copy-start(s32[256]{0:T(256)} %param.11) | copy-start | bytes 3076
  68.3 5.7 %slice-start = ((s8[4718592]{0:T(1024)(128)(4,1)}), s8[4194304]{0:T(1024)(128)(4,1)S(1)}, s32[]{:S(2)}) async-start(s8[4718592]{0:T(1024)(128)(4,1)} %bitcast.41), calls=%async_computation.1 | async-start | bytes 8388608
  68.3 5.7 %slice-start.1 = ((s8[4718592]{0:T(1024)(128)(4,1)}), s8[524288]{0:T(1024)(128)(4,1)S(1)}, s32[]{:S(2)}) async-start(s8[4718592]{0:T(1024)(128)(4,1)} %bitcast.41), calls=%async_computation.2 | async-start | bytes 1048576
  74.1 4.3 %copy-start.1 = (bf16[512,4096]{1,0:T(8,128)(2,1)S(1)}, bf16[512,4096]{1,0:T(8,128)(2,1)}, u32[]{:S(2)}) copy-start(bf16[512,4096]{1,0:T(8,128)(2,1)} %param.15) | copy-start | bytes 12582916
Sparse Core Ops, SparseCore 0:
  9.5 58.7 all-gather.2
where the time goes:
time: 88.3 us; the launch traced here: 88 us
  waiting for transfers between devices  32.6 us (37%)
  blocking collectives  23.2 us (26%)
  matrix products  15.4 us (17%)
  between operations  13.5 us (15%)
  local copies, waits for them, and re-layouts  2.52 us (3%)
    all_gather x1, waiting for transfers between devices, shards(): piece = lax.all_gather(cache, 'col', axis=0, tiled=True)  31.8 us
    all_gather x1, blocking collectives, shards(): piece_docs = lax.all_gather(key_docs, 'col', axis=0, tiled=True)  23.2 us
    dot_general x1, matrix products, shards(): jnp.einsum('rc,kc->rk', q_whole, wide_piece, precision=highest) * scale  4.96 us
    dot_general x1, matrix products, shards(): added = jnp.dot(weights, wide_piece[:, :R], precision=highest)  4.28 us
    dot_general x1, matrix products, shards(): jnp.einsum('qhd,rhd->qhr', q_flat, w_uk.astype(jnp.float32).reshape(R, H,...  3.38 us
    dot_general x1, matrix products, shards(): jnp.einsum('qhr,rhv->qhv', mixed, w_uv.reshape(R, H, DV).astype(jnp.float...  2.82 us
  transfers between devices with their start and end apart: 1, of which 1 were waited for; matrix products, arithmetic and copies ran while one was open for 7% of the time, Pallas kernels for 0%

commit v1 on v0

v1 whole, which is shorter than its diff:
```python
import functools
import math

import jax
import jax.numpy as jnp
from jax import lax
from jax.experimental import pallas as pl
from jax.experimental.pallas import tpu as pltpu
from jax.sharding import PartitionSpec as P

H = 32
DN = 128
DR = 64
DV = 128
R = 512
PLANE = 4
QUARTERS = 4
STEPS = H // QUARTERS
CHUNKS = 2
MESH = pl.DeviceIdType.MESH
F32 = jnp.float32
BF16 = jnp.bfloat16


def cut(rows):
    units = rows // 16
    ends = [16 * (units * i // CHUNKS) for i in range(CHUNKS + 1)]
    return [(a, b - a) for a, b in zip(ends[:-1], ends[1:])]


def split(x):
    high = x.astype(BF16)
    return high, (x - high.astype(F32)).astype(BF16)


def kernel(
    zs, batches, nope_ref, rope_ref, cache_ref, kdocs_ref, qdocs_ref, qpos_ref, wuk_hbm, wuv_hbm, out_ref,
    wuk, wuv, kbuf, qtmp, qbuf, abuf, sbuf, pbuf, accb, obuf, rbuf,
    wsem, csend, crecv, xsend, xrecv, fsend, frecv, qsend, qrecv, osend, orecv,
):
    me = lax.axis_index("col")
    t = lax.rem(me, PLANE)
    zi = lax.div(me, PLANE)
    base = me - t
    mate_t = t + 1 - 2 * lax.rem(t, 2)
    cross_t = t + 2 - 4 * lax.div(t, 2)
    far_t = mate_t + 2 - 4 * lax.div(mate_t, 2)
    mate, cross = base + mate_t, base + cross_t
    peers = [lax.rem(zi + d, zs) * PLANE + t for d in range(zs)]

    barrier = pltpu.get_barrier_semaphore()
    for other in [mate, cross] + peers[1:]:
        pl.semaphore_signal(barrier, inc=1, device_id={"col": other}, device_id_type=MESH)

    load_uk = pltpu.make_async_copy(wuk_hbm, wuk, wsem.at[0])
    load_uv = pltpu.make_async_copy(wuv_hbm, wuv, wsem.at[1])
    load_uk.start()
    load_uv.start()

    tokens = cache_ref.shape[0]
    own = nope_ref.shape[0]
    rows = QUARTERS * own
    wide = STEPS * DN
    turn = STEPS * DR
    kbuf[0, :tokens, :R] = cache_ref[:, :R]
    krope = cache_ref[:, R:].astype(F32)
    kbuf[0, :tokens, R:] = jnp.concatenate([krope, krope], axis=1).astype(BF16)
    kbuf[0, tokens:, :tokens] = jnp.broadcast_to(kdocs_ref[...].astype(F32), (16, tokens)).astype(BF16)
    kbuf[0, tokens:, tokens:] = jnp.zeros((16, R + 2 * DR - tokens), BF16)
    nope = nope_ref[...].astype(F32)
    rope = rope_ref[...].astype(F32)
    for k in range(QUARTERS):
        qtmp[pl.ds(own * k, own), :wide] = nope[:, k * wide:(k + 1) * wide]
        qtmp[pl.ds(own * k, own), wide:wide + turn] = rope[:, k * turn:(k + 1) * turn]
    row_query = lax.broadcasted_iota(jnp.int32, (rows, 128), 0) % own
    lane = lax.broadcasted_iota(jnp.int32, (rows, 128), 1)
    meta = jnp.zeros((rows, 128), jnp.int32)
    for i in range(own):
        place = qpos_ref[i]
        told = jnp.where(lane == 0, qdocs_ref[i], jnp.where(lane == 1, place >> 7, place & 127))
        meta = jnp.where(row_query == i, told, meta)
    qtmp[:, wide + turn:] = meta.astype(F32)
    qbuf[zi] = qtmp[...].astype(BF16)

    pl.semaphore_wait(barrier, 1 + zs)

    def remote(src, dst, send, recv, to):
        return pltpu.make_async_remote_copy(
            src_ref=src, dst_ref=dst, send_sem=send, recv_sem=recv, device_id={"col": to}, device_id_type=MESH
        )

    pieces = cut(tokens + 16)
    x_copies = [
        remote(kbuf.at[0, pl.ds(a, n)], kbuf.at[2, pl.ds(a, n)], xsend.at[i], xrecv.at[i], cross)
        for i, (a, n) in enumerate(pieces)
    ]
    relays = [
        remote(kbuf.at[2, pl.ds(a, n)], kbuf.at[3, pl.ds(a, n)], fsend.at[i], frecv.at[i], mate)
        for i, (a, n) in enumerate(pieces)
    ]
    q_copies = [remote(qbuf.at[zi], qbuf.at[zi], qsend.at[d], qrecv.at[d], peers[d]) for d in range(1, zs)]
    mate_copy = remote(kbuf.at[0], kbuf.at[1], csend.at[0], crecv.at[0], mate)
    for c in x_copies:
        c.start()
    for c in q_copies:
        c.start()
    mate_copy.start()

    high_rows = zs * rows
    steps = STEPS // batches
    batch_rows = steps * high_rows
    quarter = lax.broadcasted_iota(jnp.int32, (high_rows, 128), 0) % rows // own
    pick = [quarter == k for k in range(QUARTERS)]
    pick_low = [jnp.where(p, 1.0, 0.0).astype(BF16) for p in pick]
    parity = lax.broadcasted_iota(jnp.int32, (high_rows, 128), 1) // DR
    side = [jnp.where(parity == i, 1.0, 0.0).astype(BF16) for i in range(2)]

    for c in q_copies:
        c.wait_recv()
    load_uk.wait()
    for h in range(STEPS):
        b, j = h // steps, h % steps
        q = qbuf[:, :, h * DN:(h + 1) * DN].reshape(high_rows, DN)
        spread = jnp.concatenate([q * p for p in pick_low], axis=1)
        w = jnp.concatenate([wuk[:, k * wide + h * DN:k * wide + (h + 1) * DN] for k in range(QUARTERS)], axis=1)
        absorbed = lax.dot_general(spread, w, (((1,), (1,)), ((), ())), preferred_element_type=F32)
        high, low = split(absorbed)
        at = wide + (h // 2) * 2 * DR
        turned = qbuf[:, :, at:at + 2 * DR].reshape(high_rows, 2 * DR) * side[h % 2]
        span = pl.ds(j * high_rows, high_rows)
        abuf[b, 0, span, :R] = high
        abuf[b, 1, span, :R] = low
        abuf[b, 0, span, R:] = turned
        abuf[b, 1, span, R:] = jnp.zeros_like(turned)

    told = qbuf[:, :, wide + turn:].reshape(high_rows, 128).astype(F32)
    q_doc = told[:, 0:1]
    q_place = told[:, 1:2] * 128.0 + told[:, 2:3]
    factor = math.log2(math.e) / math.sqrt(DN + DR)

    def score(slot, piece_t):
        k_doc = kbuf[slot, tokens:, :tokens].astype(F32)[0:1]
        first = (base + piece_t) * tokens
        k_place = (lax.broadcasted_iota(jnp.int32, (1, tokens), 1) + first).astype(F32)
        visible = (k_doc == q_doc) & (k_place <= q_place)
        keys = kbuf[slot, :tokens, :]
        for b in range(batches):
            both = lax.dot_general(
                abuf[b].reshape(2 * batch_rows, R + 2 * DR), keys, (((1,), (1,)), ((), ())),
                preferred_element_type=F32,
            )
            for j in range(steps):
                a = j * high_rows
                s = (both[a:a + high_rows] + both[batch_rows + a:batch_rows + a + high_rows]) * factor
                sbuf[b, pl.ds(a, high_rows), slot * tokens:(slot + 1) * tokens] = jnp.where(visible, s, -1e30)

    score(0, t)
    mate_copy.wait_recv()
    score(1, mate_t)
    for c, f in zip(x_copies, relays):
        c.wait_recv()
        f.start()
    score(2, cross_t)
    for f in relays:
        f.wait_recv()
    score(3, far_t)

    stat_lane = lax.broadcasted_iota(jnp.int32, (high_rows, 128), 1)
    o_copies = []
    for b in range(batches):
        stats = jnp.zeros((high_rows, 128), F32)
        for j in range(steps):
            span = pl.ds(j * high_rows, high_rows)
            s = sbuf[b, span, :]
            top = jnp.max(s, axis=1, keepdims=True)
            p = jnp.exp2(s - top)
            total = jnp.sum(p, axis=1, keepdims=True)
            high, low = split(p)
            pbuf[0, span, :] = high
            pbuf[1, span, :] = low
            stats = jnp.where(stat_lane == j, top, jnp.where(stat_lane == 64 + j, total, stats))
        probs = pbuf[...].reshape(2 * batch_rows, PLANE * tokens)
        mixed = jnp.dot(
            probs, kbuf[:, :tokens, :R].reshape(PLANE * tokens, R), preferred_element_type=F32
        )
        accb[...] = mixed[:batch_rows] + mixed[batch_rows:]
        if b == 0:
            load_uv.wait()
        for j in range(steps):
            h = b * steps + j
            high, low = split(accb[pl.ds(j * high_rows, high_rows), :])
            w = jnp.concatenate([wuv[:, k * wide + h * DV:k * wide + (h + 1) * DV] for k in range(QUARTERS)], axis=1)
            up = jnp.dot(jnp.concatenate([high, low], axis=0), w, preferred_element_type=F32)
            up = up[:high_rows] + up[high_rows:]
            mine = jnp.zeros((high_rows, DV), F32)
            for k in range(QUARTERS):
                mine = jnp.where(pick[k], up[:, k * DV:(k + 1) * DV], mine)
            obuf[b, :, :, j * DV:(j + 1) * DV] = mine.reshape(zs, rows, DV)
        obuf[b, :, :, steps * DV:] = stats.reshape(zs, rows, 128)
        for d in range(1, zs):
            to = lax.rem(zi + d, zs)
            c = remote(obuf.at[b, to], rbuf.at[b, d], osend.at[b, d], orecv.at[b, d], peers[d])
            c.start()
            o_copies.append(c)

    for b in range(batches):
        for c in o_copies[b * (zs - 1):(b + 1) * (zs - 1)]:
            c.wait_recv()
        mine = obuf[b, zi]
        found = [mine] + [rbuf[b, d] for d in range(1, zs)]
        stats = [f[:, steps * DV:] for f in found]
        top = functools.reduce(jnp.maximum, stats)
        share = [jnp.exp2(s - top) for s in stats]
        for j in range(steps):
            numer = jnp.zeros((rows, DV), F32)
            denom = jnp.zeros((rows, 1), F32)
            for f, s, w in zip(found, stats, share):
                part = w[:, j:j + 1]
                numer += part * f[:, j * DV:(j + 1) * DV]
                denom += part * s[:, 64 + j:65 + j]
            out_ref[:, (b * steps + j) * DV:(b * steps + j + 1) * DV] = numer / denom

    for c in [mate_copy] + x_copies + relays + q_copies + o_copies:
        c.wait_send()


def solution(mesh):
    zs = mesh.shape["col"] // PLANE
    batches = 2 if zs <= 8 else 8
    steps = STEPS // batches

    def shards(query_nope, query_rope, cache, key_docs, query_docs, query_pos, w_uk, w_uv):
        own = query_nope.shape[0]
        rows = QUARTERS * own
        tokens = cache.shape[0]
        payload = STEPS * (DN + DR) + 128
        high_rows = zs * rows
        batch_rows = steps * high_rows
        sem = pltpu.SemaphoreType.DMA
        vmem = pl.BlockSpec(memory_space=pltpu.VMEM)
        smem = pl.BlockSpec(memory_space=pltpu.SMEM)
        hbm = pl.BlockSpec(memory_space=pl.ANY)
        out = pl.pallas_call(
            functools.partial(kernel, zs, batches),
            out_shape=jax.ShapeDtypeStruct((rows, STEPS * DV), F32),
            in_specs=[vmem, vmem, vmem, vmem, smem, smem, hbm, hbm],
            out_specs=vmem,
            scratch_shapes=[
                pltpu.VMEM(w_uk.shape, BF16),
                pltpu.VMEM(w_uv.shape, BF16),
                pltpu.VMEM((PLANE, tokens + 16, R + 2 * DR), BF16),
                pltpu.VMEM((rows, payload), F32),
                pltpu.VMEM((zs, rows, payload), BF16),
                pltpu.VMEM((batches, 2, batch_rows, R + 2 * DR), BF16),
                pltpu.VMEM((batches, batch_rows, PLANE * tokens), F32),
                pltpu.VMEM((2, batch_rows, PLANE * tokens), BF16),
                pltpu.VMEM((batch_rows, R), F32),
                pltpu.VMEM((batches, zs, rows, steps * DV + 128), F32),
                pltpu.VMEM((batches, zs, rows, steps * DV + 128), F32),
                sem((2,)),
                sem((1,)),
                sem((1,)),
                sem((CHUNKS,)),
                sem((CHUNKS,)),
                sem((CHUNKS,)),
                sem((CHUNKS,)),
                sem((zs,)),
                sem((zs,)),
                sem((batches, zs)),
                sem((batches, zs)),
            ],
            compiler_params=pltpu.CompilerParams(
                collective_id=0, has_side_effects=True, vmem_limit_bytes=60 * 1024 * 1024
            ),
        )(query_nope, query_rope, cache, key_docs.reshape(1, tokens), query_docs, query_pos, w_uk, w_uv)
        out = out.reshape(QUARTERS, own, STEPS * DV).transpose(1, 0, 2)
        return out.reshape(own, H * DV).astype(BF16)

    shared = P(("ga", "col"), None)
    flat = P(("ga", "col"))
    return jax.shard_map(
        shards,
        mesh=mesh,
        in_specs=(shared, shared, shared, flat, flat, flat, P(), P()),
        out_specs=shared,
        check_vma=False,
    )
```

time: 88.3 us -> 31.2 us (0.35)
  waiting for transfers between devices: 32.6 us -> 0 us
  Pallas kernels: 0 us -> 27.6 us
  blocking collectives: 23.2 us -> 0 us
  matrix products: 15.4 us -> 0 us
  between operations: 13.5 us -> 0.01 us
    all_gather x1 -> x0, waiting for transfers between devices: 31.8 us -> none  [shards(): piece = lax.all_gather(cache, 'col', axis=0, tiled=True)]
    pallas_call x0 -> x1, Pallas kernels: none -> 27.6 us  [shards(): pl.pallas_call(functools.partial(kernel, zs, batches), out_shape=jax.Shap...]
    all_gather x1 -> x0, blocking collectives: 23.2 us -> none  [shards(): piece_docs = lax.all_gather(key_docs, 'col', axis=0, tiled=True)]
    dot_general x4 -> x0, matrix products: 15.4 us -> none  [the longest x1 4.96 us: shards(): jnp.einsum('rc,kc->rk', q_whole, wide_piece, precision=highest) * scale]
    unnamed x10 -> x1, local copies, waits for them, and re-layouts: 0.02 us -> 1.84 us
    broadcast_in_dim x2 -> x0, local copies, waits for them, and re-layouts: 1.45 us -> none  [the longest x1 0.72 us: shards(): row_docs = jnp.repeat(query_docs, H)]
  transfers between devices with their start and end apart: 1 -> 0, of which waited for: 1 -> 0; matrix products, arithmetic and copies ran while one was open for 7% -> 0% of each run, Pallas kernels for 0% -> 0%
where the time goes in v1:
time: 31.2 us; the launch traced here: 31 us
  Pallas kernels  27.6 us (88%)
  local copies, waits for them, and re-layouts  2.48 us (8%)
  other arithmetic  0.85 us (3%)
    pallas_call x1, Pallas kernels, shards(): pl.pallas_call(functools.partial(kernel, zs, batches), out_shape=jax.Shap...  27.6 us
    unnamed x1, local copies, waits for them, and re-layouts  1.84 us
    convert_element_type x1, other arithmetic, shards(): return out.reshape(own, H * DV).astype(BF16)  0.85 us
    convert_element_type x1, local copies, waits for them, and re-layouts, shards(): return out.reshape(own, H * DV).astype(BF16)  0.64 us

profile of v1, /device:TPU:0, one launch (start us, length us, event | category | flops | bytes accessed | tf_op | source)
XLA Modules:
  0.0 31.0 jit_solution(2358871983757392575)
XLA Ops:
  0.0 1.8 %copy.9.cache_ref = bf16[256,576]{1,0:T(8,128)(2,1)} copy(bf16[256,576]{0,1:T(8,128)(2,1)} %param.10) | data formatting | bytes 589824 | tf_op args[2]
  1.8 27.6 %shard_map.82 = f32[16,1024]{1,0:T(8,128)} custom-call(bf16[4,4096]{1,0:T(4,128)(2,1)} %nope_ref.1, bf16[4,2048]{1,0:T(4,128)(2,1)} %rope_ref.1, bf16[256,576]{1,0:T(8,128)(2,1)} %copy.9.cache_ref, s32[1,256]{1,0:T(1,128)} %bitcast.4, s32[4]{0:T(128)} %qdocs_ref.1, s32[4]{0:T(128)} %qpos_ref.1, bf16[512,4096]{1,0:T(8,128)(2,1)} %wuk_hbm.1, ...), custom_call_target="tpu_custom_call" | custom-call | tf_op jit(solution)/shard_map/pallas_call | solution.py:243
  29.5 0.8 %convert_element_type.12 = bf16[16,1024]{1,0:T(8,128)(2,1)S(1)} convert(f32[16,1024]{1,0:T(8,128)} %shard_map.82) | non-fusion elementwise | flops 16384 | bytes 98304 | tf_op jit(solution)/shard_map/convert_element_type | solution.py:277
  30.3 0.6 %convert_element_type.13 = bf16[4,4,1024]{2,1,0:T(4,128)(2,1)} reshape(bf16[16,1024]{1,0:T(8,128)(2,1)S(1)} %convert_element_type.12) | data formatting | bytes 65536 | tf_op jit(solution)/shard_map/convert_element_type | solution.py:277

commit v2 on v1

--- a/solution.py
+++ b/solution.py
@@ -34,9 +34,9 @@
 
 
 def kernel(
-    zs, batches, nope_ref, rope_ref, cache_ref, kdocs_ref, qdocs_ref, qpos_ref, wuk_hbm, wuv_hbm, out_ref,
-    wuk, wuv, kbuf, qtmp, qbuf, abuf, sbuf, pbuf, accb, obuf, rbuf,
-    wsem, csend, crecv, xsend, xrecv, fsend, frecv, qsend, qrecv, osend, orecv,
+    zs, batches, groups, nope_ref, rope_ref, cache_ref, kdocs_ref, qdocs_ref, qpos_ref, wuk_hbm, wuv_hbm, out_ref,
+    wuk, wuv, kbuf, qtmp, qbuf, abuf, sbuf, pbuf, accb, obuf, rbuf, tbuf, trbuf,
+    wsem, csend, crecv, xsend, xrecv, fsend, frecv, qsend, qrecv, osend, orecv, tsend, trecv,
 ):
     me = lax.axis_index("col")
     t = lax.rem(me, PLANE)
@@ -57,16 +57,13 @@
     load_uk.start()
     load_uv.start()
 
-    tokens = cache_ref.shape[0]
+    tokens = cache_ref.shape[1]
     own = nope_ref.shape[0]
     rows = QUARTERS * own
     wide = STEPS * DN
     turn = STEPS * DR
-    kbuf[0, :tokens, :R] = cache_ref[:, :R]
-    krope = cache_ref[:, R:].astype(F32)
-    kbuf[0, :tokens, R:] = jnp.concatenate([krope, krope], axis=1).astype(BF16)
-    kbuf[0, tokens:, :tokens] = jnp.broadcast_to(kdocs_ref[...].astype(F32), (16, tokens)).astype(BF16)
-    kbuf[0, tokens:, tokens:] = jnp.zeros((16, R + 2 * DR - tokens), BF16)
+    kbuf[0, :R + DR] = cache_ref[...]
+    kbuf[0, R + DR:] = jnp.broadcast_to(kdocs_ref[...].astype(F32), (16, tokens)).astype(BF16)
     nope = nope_ref[...].astype(F32)
     rope = rope_ref[...].astype(F32)
     for k in range(QUARTERS):
@@ -89,7 +86,7 @@
             src_ref=src, dst_ref=dst, send_sem=send, recv_sem=recv, device_id={"col": to}, device_id_type=MESH
         )
 
-    pieces = cut(tokens + 16)
+    pieces = cut(R + DR + 16)
     x_copies = [
         remote(kbuf.at[0, pl.ds(a, n)], kbuf.at[2, pl.ds(a, n)], xsend.at[i], xrecv.at[i], cross)
         for i, (a, n) in enumerate(pieces)
@@ -109,6 +106,8 @@
     high_rows = zs * rows
     steps = STEPS // batches
     batch_rows = steps * high_rows
+    group_steps = STEPS // groups
+    group_rows = group_steps * high_rows
     quarter = lax.broadcasted_iota(jnp.int32, (high_rows, 128), 0) % rows // own
     pick = [quarter == k for k in range(QUARTERS)]
     pick_low = [jnp.where(p, 1.0, 0.0).astype(BF16) for p in pick]
@@ -119,7 +118,7 @@
         c.wait_recv()
     load_uk.wait()
     for h in range(STEPS):
-        b, j = h // steps, h % steps
+        g, j = h // group_steps, h % group_steps
         q = qbuf[:, :, h * DN:(h + 1) * DN].reshape(high_rows, DN)
         spread = jnp.concatenate([q * p for p in pick_low], axis=1)
         w = jnp.concatenate([wuk[:, k * wide + h * DN:k * wide + (h + 1) * DN] for k in range(QUARTERS)], axis=1)
@@ -128,10 +127,10 @@
         at = wide + (h // 2) * 2 * DR
         turned = qbuf[:, :, at:at + 2 * DR].reshape(high_rows, 2 * DR) * side[h % 2]
         span = pl.ds(j * high_rows, high_rows)
-        abuf[b, 0, span, :R] = high
-        abuf[b, 1, span, :R] = low
-        abuf[b, 0, span, R:] = turned
-        abuf[b, 1, span, R:] = jnp.zeros_like(turned)
+        abuf[g, 0, span, :R] = high
+        abuf[g, 1, span, :R] = low
+        abuf[g, 0, span, R:] = turned
+        abuf[g, 1, span, R:] = jnp.zeros_like(turned)
 
     told = qbuf[:, :, wide + turn:].reshape(high_rows, 128).astype(F32)
     q_doc = told[:, 0:1]
@@ -139,20 +138,17 @@
     factor = math.log2(math.e) / math.sqrt(DN + DR)
 
     def score(slot, piece_t):
-        k_doc = kbuf[slot, tokens:, :tokens].astype(F32)[0:1]
+        k_doc = kbuf[slot, R + DR:, :].astype(F32)[0:1]
         first = (base + piece_t) * tokens
         k_place = (lax.broadcasted_iota(jnp.int32, (1, tokens), 1) + first).astype(F32)
         visible = (k_doc == q_doc) & (k_place <= q_place)
-        keys = kbuf[slot, :tokens, :]
-        for b in range(batches):
-            both = lax.dot_general(
-                abuf[b].reshape(2 * batch_rows, R + 2 * DR), keys, (((1,), (1,)), ((), ())),
-                preferred_element_type=F32,
-            )
-            for j in range(steps):
+        keys = jnp.concatenate([kbuf[slot, :R + DR], kbuf[slot, R:R + DR]], axis=0)
+        for g in range(groups):
+            both = jnp.dot(abuf[g].reshape(2 * group_rows, R + 2 * DR), keys, preferred_element_type=F32)
+            for j in range(group_steps):
                 a = j * high_rows
-                s = (both[a:a + high_rows] + both[batch_rows + a:batch_rows + a + high_rows]) * factor
-                sbuf[b, pl.ds(a, high_rows), slot * tokens:(slot + 1) * tokens] = jnp.where(visible, s, -1e30)
+                s = (both[a:a + high_rows] + both[group_rows + a:group_rows + a + high_rows]) * factor
+                sbuf[g * group_steps + j, :, slot * tokens:(slot + 1) * tokens] = jnp.where(visible, s, -1e30)
 
     score(0, t)
     mate_copy.wait_recv()
@@ -167,22 +163,33 @@
 
     stat_lane = lax.broadcasted_iota(jnp.int32, (high_rows, 128), 1)
     o_copies = []
+    t_copies = []
+    stats = jnp.zeros((high_rows, 128), F32)
     for b in range(batches):
-        stats = jnp.zeros((high_rows, 128), F32)
         for j in range(steps):
             span = pl.ds(j * high_rows, high_rows)
-            s = sbuf[b, span, :]
+            h = b * steps + j
+            s = sbuf[h]
             top = jnp.max(s, axis=1, keepdims=True)
             p = jnp.exp2(s - top)
             total = jnp.sum(p, axis=1, keepdims=True)
             high, low = split(p)
             pbuf[0, span, :] = high
             pbuf[1, span, :] = low
-            stats = jnp.where(stat_lane == j, top, jnp.where(stat_lane == 64 + j, total, stats))
-        probs = pbuf[...].reshape(2 * batch_rows, PLANE * tokens)
-        mixed = jnp.dot(
-            probs, kbuf[:, :tokens, :R].reshape(PLANE * tokens, R), preferred_element_type=F32
-        )
+            stats = jnp.where(stat_lane == h, top, jnp.where(stat_lane == 64 + h, total, stats))
+        if b == batches - 1:
+            tbuf[...] = stats.reshape(zs, rows, 128)
+            for d in range(1, zs):
+                to = lax.rem(zi + d, zs)
+                c = remote(tbuf.at[to], trbuf.at[d], tsend.at[d], trecv.at[d], peers[d])
+                c.start()
+                t_copies.append(c)
+        mixed = jnp.zeros((2 * batch_rows, R), F32)
+        for slot in range(PLANE):
+            probs = pbuf[:, :, slot * tokens:(slot + 1) * tokens].reshape(2 * batch_rows, tokens)
+            mixed += lax.dot_general(
+                probs, kbuf[slot, :R], (((1,), (1,)), ((), ())), preferred_element_type=F32
+            )
         accb[...] = mixed[:batch_rows] + mixed[batch_rows:]
         if b == 0:
             load_uv.wait()
@@ -196,37 +203,41 @@
             for k in range(QUARTERS):
                 mine = jnp.where(pick[k], up[:, k * DV:(k + 1) * DV], mine)
             obuf[b, :, :, j * DV:(j + 1) * DV] = mine.reshape(zs, rows, DV)
-        obuf[b, :, :, steps * DV:] = stats.reshape(zs, rows, 128)
         for d in range(1, zs):
             to = lax.rem(zi + d, zs)
             c = remote(obuf.at[b, to], rbuf.at[b, d], osend.at[b, d], orecv.at[b, d], peers[d])
             c.start()
             o_copies.append(c)
 
+    for c in t_copies:
+        c.wait_recv()
+    stats = [tbuf[zi]] + [trbuf[d] for d in range(1, zs)]
+    top = functools.reduce(jnp.maximum, stats)
+    share = [jnp.exp2(f - top) for f in stats]
     for b in range(batches):
         for c in o_copies[b * (zs - 1):(b + 1) * (zs - 1)]:
             c.wait_recv()
-        mine = obuf[b, zi]
-        found = [mine] + [rbuf[b, d] for d in range(1, zs)]
-        stats = [f[:, steps * DV:] for f in found]
-        top = functools.reduce(jnp.maximum, stats)
-        share = [jnp.exp2(s - top) for s in stats]
+        found = [obuf[b, zi]] + [rbuf[b, d] for d in range(1, zs)]
         for j in range(steps):
+            h = b * steps + j
             numer = jnp.zeros((rows, DV), F32)
             denom = jnp.zeros((rows, 1), F32)
             for f, s, w in zip(found, stats, share):
-                part = w[:, j:j + 1]
+                part = w[:, h:h + 1]
                 numer += part * f[:, j * DV:(j + 1) * DV]
-                denom += part * s[:, 64 + j:65 + j]
-            out_ref[:, (b * steps + j) * DV:(b * steps + j + 1) * DV] = numer / denom
-
-    for c in [mate_copy] + x_copies + relays + q_copies + o_copies:
+                denom += part * s[:, 64 + h:65 + h]
+            done = numer / denom
+            for k in range(QUARTERS):
+                out_ref[:, k * wide + h * DV:k * wide + (h + 1) * DV] = done[k * own:(k + 1) * own]
+
+    for c in [mate_copy] + x_copies + relays + q_copies + o_copies + t_copies:
         c.wait_send()
 
 
 def solution(mesh):
     zs = mesh.shape["col"] // PLANE
-    batches = 2 if zs <= 8 else 8
+    batches = 4 if zs <= 8 else 8
+    groups = 1 if zs <= 8 else 8
     steps = STEPS // batches
 
     def shards(query_nope, query_rope, cache, key_docs, query_docs, query_pos, w_uk, w_uv):
@@ -241,22 +252,24 @@
         smem = pl.BlockSpec(memory_space=pltpu.SMEM)
         hbm = pl.BlockSpec(memory_space=pl.ANY)
         out = pl.pallas_call(
-            functools.partial(kernel, zs, batches),
-            out_shape=jax.ShapeDtypeStruct((rows, STEPS * DV), F32),
+            functools.partial(kernel, zs, batches, groups),
+            out_shape=jax.ShapeDtypeStruct((own, H * DV), F32),
             in_specs=[vmem, vmem, vmem, vmem, smem, smem, hbm, hbm],
             out_specs=vmem,
             scratch_shapes=[
                 pltpu.VMEM(w_uk.shape, BF16),
                 pltpu.VMEM(w_uv.shape, BF16),
-                pltpu.VMEM((PLANE, tokens + 16, R + 2 * DR), BF16),
+                pltpu.VMEM((PLANE, R + DR + 16, tokens), BF16),
                 pltpu.VMEM((rows, payload), F32),
                 pltpu.VMEM((zs, rows, payload), BF16),
-                pltpu.VMEM((batches, 2, batch_rows, R + 2 * DR), BF16),
-                pltpu.VMEM((batches, batch_rows, PLANE * tokens), F32),
+                pltpu.VMEM((groups, 2, STEPS // groups * high_rows, R + 2 * DR), BF16),
+                pltpu.VMEM((STEPS, high_rows, PLANE * tokens), F32),
                 pltpu.VMEM((2, batch_rows, PLANE * tokens), BF16),
                 pltpu.VMEM((batch_rows, R), F32),
-                pltpu.VMEM((batches, zs, rows, steps * DV + 128), F32),
-                pltpu.VMEM((batches, zs, rows, steps * DV + 128), F32),
+                pltpu.VMEM((batches, zs, rows, steps * DV), F32),
+                pltpu.VMEM((batches, zs, rows, steps * DV), F32),
+                pltpu.VMEM((zs, rows, 128), F32),
+                pltpu.VMEM((zs, rows, 128), F32),
                 sem((2,)),
                 sem((1,)),
                 sem((1,)),
@@ -268,13 +281,14 @@
                 sem((zs,)),
                 sem((batches, zs)),
                 sem((batches, zs)),
+                sem((zs,)),
+                sem((zs,)),
             ],
             compiler_params=pltpu.CompilerParams(
                 collective_id=0, has_side_effects=True, vmem_limit_bytes=60 * 1024 * 1024
             ),
-        )(query_nope, query_rope, cache, key_docs.reshape(1, tokens), query_docs, query_pos, w_uk, w_uv)
-        out = out.reshape(QUARTERS, own, STEPS * DV).transpose(1, 0, 2)
-        return out.reshape(own, H * DV).astype(BF16)
+        )(query_nope, query_rope, cache.T, key_docs.reshape(1, tokens), query_docs, query_pos, w_uk, w_uv)
+        return out.astype(BF16)
 
     shared = P(("ga", "col"), None)
     flat = P(("ga", "col"))

time: 31.2 us -> 29 us (0.929)
  local copies, waits for them, and re-layouts: 2.48 us -> 0 us
  other arithmetic: 0.85 us -> 1.47 us
    unnamed x1 -> x0, local copies, waits for them, and re-layouts: 1.84 us -> none
    convert_element_type x1 -> x0, local copies, waits for them, and re-layouts: 0.64 us -> none  [shards(): return out.reshape(own, H * DV).astype(BF16)]
    convert_element_type x1, other arithmetic: 0.85 us -> 1.47 us  [shards(): return out.astype(BF16)]
    pallas_call x1, Pallas kernels: 27.6 us -> 27.3 us  [shards(): pl.pallas_call(functools.partial(kernel, zs, batches, groups), out_shape=...]
where the time goes in v2:
time: 29 us; the launch traced here: 28.8 us
  Pallas kernels  27.3 us (94%)
  other arithmetic  1.47 us (5%)
    pallas_call x1, Pallas kernels, shards(): pl.pallas_call(functools.partial(kernel, zs, batches, groups), out_shape=...  27.3 us
    convert_element_type x1, other arithmetic, shards(): return out.astype(BF16)  1.47 us

profile of v2, /device:TPU:0, one launch (start us, length us, event | category | flops | bytes accessed | tf_op | source)
XLA Modules:
  0.0 28.8 jit_solution(2655591995270685859)
XLA Ops:
  0.0 27.3 %shard_map.82 = f32[4,4096]{1,0:T(4,128)} custom-call(bf16[4,4096]{1,0:T(4,128)(2,1)} %nope_ref.1, bf16[4,2048]{1,0:T(4,128)(2,1)} %rope_ref.1, bf16[576,256]{1,0:T(8,128)(2,1)} %bitcast.2, s32[1,256]{1,0:T(1,128)} %bitcast.3, s32[4]{0:T(128)} %qdocs_ref.1, s32[4]{0:T(128)} %qpos_ref.1, bf16[512,4096]{1,0:T(8,128)(2,1)} %wuk_hbm.1, bf16[512,4096]{1,0:T(8,128)(2,1)} %wuv_hbm.1), custom_call_target="tpu_custom_call" | custom-call | tf_op jit(solution)/shard_map/pallas_call | solution.py:254
  27.3 1.5 %convert_element_type.3 = bf16[4,4096]{1,0:T(4,128)(2,1)} convert(f32[4,4096]{1,0:T(4,128)} %shard_map.82) | non-fusion elementwise | flops 16384 | bytes 98304 | tf_op jit(solution)/shard_map/convert_element_type | solution.py:291

commit v3 on v2

--- a/solution.py
+++ b/solution.py
@@ -16,7 +16,7 @@
 PLANE = 4
 QUARTERS = 4
 STEPS = H // QUARTERS
-CHUNKS = 2
+CHUNKS = 4
 MESH = pl.DeviceIdType.MESH
 F32 = jnp.float32
 BF16 = jnp.bfloat16
@@ -114,10 +114,18 @@
     parity = lax.broadcasted_iota(jnp.int32, (high_rows, 128), 1) // DR
     side = [jnp.where(parity == i, 1.0, 0.0).astype(BF16) for i in range(2)]
 
+    def relay(i):
+        x_copies[i].wait_recv()
+        relays[i].start()
+
+    relay(0)
+    relay(1)
     for c in q_copies:
         c.wait_recv()
     load_uk.wait()
     for h in range(STEPS):
+        if h == STEPS // 2:
+            relay(2)
         g, j = h // group_steps, h % group_steps
         q = qbuf[:, :, h * DN:(h + 1) * DN].reshape(high_rows, DN)
         spread = jnp.concatenate([q * p for p in pick_low], axis=1)
@@ -151,11 +159,9 @@
                 sbuf[g * group_steps + j, :, slot * tokens:(slot + 1) * tokens] = jnp.where(visible, s, -1e30)
 
     score(0, t)
+    relay(3)
     mate_copy.wait_recv()
     score(1, mate_t)
-    for c, f in zip(x_copies, relays):
-        c.wait_recv()
-        f.start()
     score(2, cross_t)
     for f in relays:
         f.wait_recv()
@@ -165,7 +171,8 @@
     o_copies = []
     t_copies = []
     stats = jnp.zeros((high_rows, 128), F32)
-    for b in range(batches):
+
+    def weigh(b, stats):
         for j in range(steps):
             span = pl.ds(j * high_rows, high_rows)
             h = b * steps + j
@@ -174,9 +181,16 @@
             p = jnp.exp2(s - top)
             total = jnp.sum(p, axis=1, keepdims=True)
             high, low = split(p)
-            pbuf[0, span, :] = high
-            pbuf[1, span, :] = low
+            pbuf[b % 2, 0, span, :] = high
+            pbuf[b % 2, 1, span, :] = low
             stats = jnp.where(stat_lane == h, top, jnp.where(stat_lane == 64 + h, total, stats))
+        return stats
+
+    load_uv.wait()
+    stats = weigh(0, stats)
+    for b in range(batches):
+        if b < batches - 1:
+            stats = weigh(b + 1, stats)
         if b == batches - 1:
             tbuf[...] = stats.reshape(zs, rows, 128)
             for d in range(1, zs):
@@ -186,13 +200,11 @@
                 t_copies.append(c)
         mixed = jnp.zeros((2 * batch_rows, R), F32)
         for slot in range(PLANE):
-            probs = pbuf[:, :, slot * tokens:(slot + 1) * tokens].reshape(2 * batch_rows, tokens)
+            probs = pbuf[b % 2, :, :, slot * tokens:(slot + 1) * tokens].reshape(2 * batch_rows, tokens)
             mixed += lax.dot_general(
                 probs, kbuf[slot, :R], (((1,), (1,)), ((), ())), preferred_element_type=F32
             )
         accb[...] = mixed[:batch_rows] + mixed[batch_rows:]
-        if b == 0:
-            load_uv.wait()
         for j in range(steps):
             h = b * steps + j
             high, low = split(accb[pl.ds(j * high_rows, high_rows), :])
@@ -228,7 +240,7 @@
                 denom += part * s[:, 64 + h:65 + h]
             done = numer / denom
             for k in range(QUARTERS):
-                out_ref[:, k * wide + h * DV:k * wide + (h + 1) * DV] = done[k * own:(k + 1) * own]
+                out_ref[:, k * wide + h * DV:k * wide + (h + 1) * DV] = done[k * own:(k + 1) * own].astype(BF16)
 
     for c in [mate_copy] + x_copies + relays + q_copies + o_copies + t_copies:
         c.wait_send()
@@ -253,7 +265,7 @@
         hbm = pl.BlockSpec(memory_space=pl.ANY)
         out = pl.pallas_call(
             functools.partial(kernel, zs, batches, groups),
-            out_shape=jax.ShapeDtypeStruct((own, H * DV), F32),
+            out_shape=jax.ShapeDtypeStruct((own, H * DV), BF16),
             in_specs=[vmem, vmem, vmem, vmem, smem, smem, hbm, hbm],
             out_specs=vmem,
             scratch_shapes=[
@@ -264,7 +276,7 @@
                 pltpu.VMEM((zs, rows, payload), BF16),
                 pltpu.VMEM((groups, 2, STEPS // groups * high_rows, R + 2 * DR), BF16),
                 pltpu.VMEM((STEPS, high_rows, PLANE * tokens), F32),
-                pltpu.VMEM((2, batch_rows, PLANE * tokens), BF16),
+                pltpu.VMEM((2, 2, batch_rows, PLANE * tokens), BF16),
                 pltpu.VMEM((batch_rows, R), F32),
                 pltpu.VMEM((batches, zs, rows, steps * DV), F32),
                 pltpu.VMEM((batches, zs, rows, steps * DV), F32),
@@ -288,7 +300,7 @@
                 collective_id=0, has_side_effects=True, vmem_limit_bytes=60 * 1024 * 1024
             ),
         )(query_nope, query_rope, cache.T, key_docs.reshape(1, tokens), query_docs, query_pos, w_uk, w_uv)
-        return out.astype(BF16)
+        return out
 
     shared = P(("ga", "col"), None)
     flat = P(("ga", "col"))

time: 29 us -> 28.9 us (level)
  other arithmetic: 1.47 us -> 0 us
  local copies, waits for them, and re-layouts: 0 us -> 1.39 us
    convert_element_type x1 -> x0, other arithmetic: 1.47 us -> none  [shards(): return out.astype(BF16)]
    unnamed x0 -> x1, local copies, waits for them, and re-layouts: none -> 1.39 us
where the time goes in v3:
time: 28.9 us; the launch traced here: 28.7 us
  Pallas kernels  27.3 us (94%)
  local copies, waits for them, and re-layouts  1.39 us (5%)
    pallas_call x1, Pallas kernels, shards(): pl.pallas_call(functools.partial(kernel, zs, batches, groups), out_shape=...  27.3 us
    unnamed x1, local copies, waits for them, and re-layouts  1.39 us

profile of v3, /device:TPU:0, one launch (start us, length us, event | category | flops | bytes accessed | tf_op | source)
XLA Modules:
  0.0 28.7 jit_solution(16605411191903614700)
XLA Ops:
  0.0 27.3 %shard_map.82 = bf16[4,4096]{1,0:T(4,128)(2,1)} custom-call(bf16[4,4096]{1,0:T(4,128)(2,1)} %nope_ref.1, bf16[4,2048]{1,0:T(4,128)(2,1)} %rope_ref.1, bf16[576,256]{1,0:T(8,128)(2,1)} %bitcast.2, s32[1,256]{1,0:T(1,128)} %bitcast.3, s32[4]{0:T(128)} %qdocs_ref.1, s32[4]{0:T(128)} %qpos_ref.1, bf16[512,4096]{1,0:T(8,128)(2,1)} %wuk_hbm.1, ...), custom_call_target="tpu_custom_call" | custom-call | tf_op jit(solution)/shard_map/pallas_call | solution.py:266
  27.3 1.4 %copy.10 = bf16[4,4096]{1,0:T(4,128)(2,1)} copy(bf16[4,4096]{1,0:T(4,128)(2,1)} %shard_map.82) | data formatting | bytes 65536
